TPU v7x, 32 devices: a whole 2x2x4 slice. The times are simulated.
32 devices in a mesh: groups: 2 (over x), rows: 16 (over z, y, core).
Axes of the slice: x: 2, y: 2, z: 4, core: 2. Of those that a mesh axis runs over, the one named last changes fastest.
Arguments:
- pair: bfloat16 [512, 256, 128], P(('groups', 'rows')), parts along dimension 0, may hold values from -6 to 6
- proj_weights: bfloat16 [6, 128, 128], replicated, may hold values from -0.5 to 0.5
- cotangent: bfloat16 [512, 256, 128], P(('groups', 'rows')), parts along dimension 0, may hold values from -8.5 to 8.5
Outputs:
- update: bfloat16 [512, 256, 128], P(('groups', 'rows')), parts along dimension 0
- pair_grad: bfloat16 [512, 256, 128], P(('groups', 'rows')), parts along dimension 0
- weight_grads: float32 [12, 128, 128], P('groups'), parts along dimension 0
There are 2 independent parts, one for each index of `groups`. A program takes and returns all parts, laid end to end along the dimension named above; an argument that names none is the same for every part. Nothing has to cross between parts.
All inputs are finite; a program needn't handle non-finite values.
Results may differ from a plain program's by a relative error of at most 0.015.
Values may be sent and summed in bfloat16 or wider, within the bound.
A program may use at most 128 MiB of HBM per device.

v0:
```python
import jax
import jax.numpy as jnp
from jax import lax
from jax.sharding import PartitionSpec as P


def layer_norm(values, along_dim):
    centred = values - jnp.mean(values, axis=along_dim, keepdims=True)
    inv_scale = lax.rsqrt(jnp.mean(centred * centred, axis=along_dim, keepdims=True) + 1e-05)
    return (centred * inv_scale, inv_scale)


def norm_backward(normed, inv_scale, upstream, along_dim):
    return (
        upstream
        - jnp.mean(upstream, axis=along_dim, keepdims=True)
        - normed * jnp.mean(upstream * normed, axis=along_dim, keepdims=True)
    ) * inv_scale


def triangle_slab(pieces):
    left_slab, right_slab = pieces
    product = lax.dot_general(
        left_slab, right_slab, (((3,), (3,)), ((0, 1), (0, 1))), preferred_element_type=jnp.float32
    )
    return (product.astype(jnp.bfloat16), left_slab, right_slab)


def edge_backward(upstream, left_slab, right_slab):
    left_part = lax.dot_general(
        upstream, right_slab, (((3,), (2,)), ((0, 1), (0, 1))), preferred_element_type=jnp.float32
    )
    right_part = lax.dot_general(
        upstream, left_slab, (((2,), (2,)), ((0, 1), (0, 1))), preferred_element_type=jnp.float32
    )
    return (left_part.astype(jnp.bfloat16), right_part.astype(jnp.bfloat16))


def body(pair, proj_weights, cotangent):
    residues = pair.shape[1]
    local_rows = pair.shape[0]
    chans = pair.shape[2]
    ranks = lax.axis_size("rows")
    slab_width = chans // ranks
    normed_in, scale_in = layer_norm(pair.astype(jnp.float32), 2)
    normed_bf = normed_in.astype(jnp.bfloat16)
    edge_pre = jnp.einsum(
        "ikd,ndc->ncik", normed_bf, proj_weights[0:4], preferred_element_type=jnp.float32
    )
    gate_pre = jnp.einsum(
        "ikd,dc->ikc", normed_bf, proj_weights[4], preferred_element_type=jnp.float32
    )
    left_sig = jax.nn.sigmoid(edge_pre[1])
    right_sig = jax.nn.sigmoid(edge_pre[3])
    left_edge = (
        (left_sig * edge_pre[0])
        .astype(jnp.bfloat16)
        .reshape(ranks, slab_width, local_rows, residues)
    )
    right_edge = (
        (right_sig * edge_pre[2])
        .astype(jnp.bfloat16)
        .reshape(ranks, slab_width, local_rows, residues)
    )
    products, left_held, right_held = triangle_slab(
        (
            lax.all_to_all(left_edge, "rows", split_axis=0, concat_axis=2, tiled=True),
            lax.all_to_all(right_edge, "rows", split_axis=0, concat_axis=2, tiled=True),
        )
    )
    regrouped = lax.all_to_all(products, "rows", split_axis=2, concat_axis=0, tiled=True).reshape(
        chans, local_rows, residues
    )
    normed_mid, scale_mid = layer_norm(regrouped.astype(jnp.float32), 0)
    mid_bf = normed_mid.astype(jnp.bfloat16)
    projected = jnp.einsum(
        "cij,cd->ijd", mid_bf, proj_weights[5], preferred_element_type=jnp.float32
    )
    gating = jax.nn.sigmoid(gate_pre)
    update = (gating * projected).astype(jnp.bfloat16)
    upstream = cotangent.astype(jnp.float32)
    gated_up = (upstream * gating).astype(jnp.bfloat16)
    gate_grad = (upstream * projected * gating * (1.0 - gating)).astype(jnp.bfloat16)
    out_weights = jnp.stack(
        [
            jnp.einsum("ikd,ikc->dc", normed_bf, gate_grad, preferred_element_type=jnp.float32),
            jnp.einsum("cij,ijd->cd", mid_bf, gated_up, preferred_element_type=jnp.float32),
        ]
    )
    mid_grad = jnp.einsum(
        "ijd,cd->cij", gated_up, proj_weights[5], preferred_element_type=jnp.float32
    )
    prod_grad = norm_backward(normed_mid, scale_mid, mid_grad, 0).astype(jnp.bfloat16)
    prod_grad = prod_grad.reshape(ranks, slab_width, local_rows, residues)
    slab_grad = lax.all_to_all(prod_grad, "rows", split_axis=0, concat_axis=2, tiled=True)
    left_part, right_part = edge_backward(slab_grad, left_held, right_held)
    left_back, right_back = (
        lax.all_to_all(left_part, "rows", split_axis=2, concat_axis=0, tiled=True),
        lax.all_to_all(right_part, "rows", split_axis=2, concat_axis=0, tiled=True),
    )
    left_full = left_back.reshape(chans, local_rows, residues).astype(jnp.float32)
    right_full = right_back.reshape(chans, local_rows, residues).astype(jnp.float32)
    edge_grad = jnp.stack(
        [
            left_full * left_sig,
            left_full * edge_pre[0] * left_sig * (1.0 - left_sig),
            right_full * right_sig,
            right_full * edge_pre[2] * right_sig * (1.0 - right_sig),
        ]
    ).astype(jnp.bfloat16)
    in_weights = jnp.einsum(
        "ikd,ncik->ndc", normed_bf, edge_grad, preferred_element_type=jnp.float32
    )
    input_grad = jnp.einsum(
        "ncik,ndc->ikd", edge_grad, proj_weights[0:4], preferred_element_type=jnp.float32
    )
    input_grad = input_grad + jnp.einsum(
        "ikc,dc->ikd", gate_grad, proj_weights[4], preferred_element_type=jnp.float32
    )
    pair_grad = norm_backward(normed_in, scale_in, input_grad, 2).astype(jnp.bfloat16)
    totals = lax.psum(
        jnp.concatenate([in_weights, out_weights], axis=0).astype(jnp.bfloat16), "rows"
    ).astype(jnp.float32)
    weight_grads = totals / residues
    return (update, pair_grad, weight_grads)


def solution(mesh):
    in_specs = (P(("groups", "rows"), None, None), P(), P(("groups", "rows"), None, None))
    out_specs = (
        P(("groups", "rows"), None, None),
        P(("groups", "rows"), None, None),
        P("groups", None, None),
    )
    return jax.shard_map(body, mesh=mesh, in_specs=in_specs, out_specs=out_specs, check_vma=False)
```

profile of v0, /device:TPU:0, one launch (start us, length us, event | category | flops | bytes accessed | tf_op | source)
XLA Modules:
  0.0 318.2 jit_solution(738744233146156121)
XLA Ops:
  7.2 1.5 copy.69
  11.7 2.0 copy-done
  14.8 7.4 %all-to-all-start.1 = ((bf16[16,8,16,256]{3,1,2,0:T(8,128)(2,1)}), bf16[16,8,16,256]{3,1,2,0:T(8,128)(2,1)S(1)}, u32[]{:S(2)}, u32[]{:S(2)}) async-start(bf16[16,8,16,256]{3,1,2,0:T(8,128)(2,1)} %copy.75), calls=%async_computation.1 | async-start | bytes 2097152 | tf_op jit(solution)/shard_map/all_to_all | solution.py:68
  23.3 21.9 %all-to-all-done.1 = bf16[16,8,16,256]{3,1,2,0:T(8,128)(2,1)S(1)} async-done(((bf16[16,8,16,256]{3,1,2,0:T(8,128)(2,1)}), bf16[16,8,16,256]{3,1,2,0:T(8,128)(2,1)S(1)}, u32[]{:S(2)}, u32[]{:S(2)}) %all-to-all-start.1) | async-done | bytes 1048608 | tf_op jit(solution)/shard_map/all_to_all | solution.py:68
  45.2 6.9 %all-to-all-start = ((bf16[16,8,16,256]{3,1,2,0:T(8,128)(2,1)}), bf16[16,8,16,256]{3,1,2,0:T(8,128)(2,1)}, u32[]{:S(2)}, u32[]{:S(2)}) async-start(bf16[16,8,16,256]{3,1,2,0:T(8,128)(2,1)} %copy.73), calls=%async_computation | async-start | bytes 2097152 | tf_op jit(solution)/shard_map/all_to_all | solution.py:67
  52.3 22.8 %all-to-all-done = bf16[16,8,16,256]{3,1,2,0:T(8,128)(2,1)} async-done(((bf16[16,8,16,256]{3,1,2,0:T(8,128)(2,1)}), bf16[16,8,16,256]{3,1,2,0:T(8,128)(2,1)}, u32[]{:S(2)}, u32[]{:S(2)}) %all-to-all-start) | async-done | bytes 1048608 | tf_op jit(solution)/shard_map/all_to_all | solution.py:67
  77.6 31.5 %all_to_all.72 = bf16[1,8,256,256]{3,1,0,2:T(8,128)(2,1)S(1)} all-to-all(bf16[1,8,256,256]{3,1,0,2:T(8,128)(2,1)S(1)} %copy.77), channel_id=1, replica_groups=mesh['groups'=2,'rows'=16] {'rows'}, dimensions={2} | all-to-all | bytes 2097152 | tf_op jit(solution)/shard_map/all_to_all | solution.py:71
  111.6 2.5 fusion.13
  114.1 1.6 bitcast_reduce_fusion
  115.8 1.6 fusion.47
  117.5 29.8 %all_to_all.73 = bf16[16,8,16,256]{3,1,2,0:T(8,128)(2,1)S(1)} all-to-all(bf16[16,8,16,256]{3,1,2,0:T(8,128)(2,1)S(1)} %copy.82), channel_id=1, replica_groups=mesh['groups'=2,'rows'=16] {'rows'}, dimensions={0} | all-to-all | bytes 2097152 | tf_op jit(solution)/shard_map/all_to_all | solution.py:95
  149.0 1.6 copy.84
  150.6 5.0 %all-to-all-start.4 = ((bf16[1,8,256,256]{3,1,0,2:T(8,128)(2,1)}), bf16[1,8,256,256]{3,1,0,2:T(8,128)(2,1)}, u32[]{:S(2)}, u32[]{:S(2)}) async-start(bf16[1,8,256,256]{3,1,0,2:T(8,128)(2,1)} %copy.84), calls=%async_computation.4 | async-start | bytes 2097152 | tf_op jit(solution)/shard_map/all_to_all | solution.py:98
  155.6 2.0 fusion.36
  157.7 1.6 copy.87
  159.3 19.3 %all-to-all-done.4 = bf16[1,8,256,256]{3,1,0,2:T(8,128)(2,1)} async-done(((bf16[1,8,256,256]{3,1,0,2:T(8,128)(2,1)}), bf16[1,8,256,256]{3,1,0,2:T(8,128)(2,1)}, u32[]{:S(2)}, u32[]{:S(2)}) %all-to-all-start.4) | async-done | bytes 1048608 | tf_op jit(solution)/shard_map/all_to_all | solution.py:98
  178.6 6.9 %all-to-all-start.5 = ((bf16[1,8,256,256]{3,1,0,2:T(8,128)(2,1)}), bf16[1,8,256,256]{3,1,0,2:T(8,128)(2,1)}, u32[]{:S(2)}, u32[]{:S(2)}) async-start(bf16[1,8,256,256]{3,1,0,2:T(8,128)(2,1)} %copy.87), calls=%async_computation.5 | async-start | bytes 2097152 | tf_op jit(solution)/shard_map/all_to_all | solution.py:99
  185.8 2.0 fusion.43
  187.8 2.9 fusion.42
  190.7 17.8 %all-to-all-done.5 = bf16[1,8,256,256]{3,1,0,2:T(8,128)(2,1)} async-done(((bf16[1,8,256,256]{3,1,0,2:T(8,128)(2,1)}), bf16[1,8,256,256]{3,1,0,2:T(8,128)(2,1)}, u32[]{:S(2)}, u32[]{:S(2)}) %all-to-all-start.5) | async-done | bytes 1048608 | tf_op jit(solution)/shard_map/all_to_all | solution.py:99
  208.5 5.0 %fusion.24 = (bf16[1,128,16,256]{3,1,0,2:T(8,128)(2,1)S(1)}, bf16[1,128,16,256]{3,1,0,2:T(8,128)(2,1)S(1)}, bf16[1,128,16,256]{3,1,0,2:T(8,128)(2,1)S(1)}, bf16[1,128,16,256]{3,1,0,2:T(8,128)(2,1)S(1)}) fusion(f32[4,128,16,256]{3,1,0,2:T(8,128)} %copy-done, bf16[1,8,16,16,256]{4,1,3,2,0:T(8,128)(2,1)} %bitcast.53, bf16[1,8,16,16,256]{4,1,3,2,0:T(8,128)(2,1)} %bitcast.51), kind=kLoop, calls=%fused_computation.37 | loop fusion | flops 11534336 | bytes 14680064 | tf_op jit(solution)/shard_map/convert.17
  217.5 1.6 fusion.8
  219.1 2.3 copy.93
  221.3 88.2 %all-reduce.2.cloned.1.call-done = bf16[6,128,128]{1,2,0:T(8,128)(2,1)} async-done(((bf16[6,128,128]{1,2,0:T(8,128)(2,1)}), bf16[6,128,128]{1,2,0:T(8,128)(2,1)}) %all-reduce.2.cloned.1.call-update) | async-done | bytes 196624 | tf_op jit(solution)/shard_map/psum | solution.py:121
  (53 shorter events, 18.1 us)
Async XLA Ops:
  7.2 2.1 copy-start.9
  10.5 3.2 %copy-start = (f32[4,128,16,256]{3,1,0,2:T(8,128)}, f32[4,128,16,256]{3,1,0,2:T(8,128)S(1)}, u32[]{:S(2)}) copy-start(f32[4,128,16,256]{3,1,0,2:T(8,128)S(1)} %convolution_bitcast_fusion) | copy-start | bytes 25165828
  14.8 30.3 %all-to-all-start.1 = ((bf16[16,8,16,256]{3,1,2,0:T(8,128)(2,1)}), bf16[16,8,16,256]{3,1,2,0:T(8,128)(2,1)S(1)}, u32[]{:S(2)}, u32[]{:S(2)}) async-start(bf16[16,8,16,256]{3,1,2,0:T(8,128)(2,1)} %copy.75), calls=%async_computation.1 | async-start | bytes 2097152 | tf_op jit(solution)/shard_map/all_to_all | solution.py:68
  45.2 29.9 %all-to-all-start = ((bf16[16,8,16,256]{3,1,2,0:T(8,128)(2,1)}), bf16[16,8,16,256]{3,1,2,0:T(8,128)(2,1)}, u32[]{:S(2)}, u32[]{:S(2)}) async-start(bf16[16,8,16,256]{3,1,2,0:T(8,128)(2,1)} %copy.73), calls=%async_computation | async-start | bytes 2097152 | tf_op jit(solution)/shard_map/all_to_all | solution.py:67
  52.3 24.7 %copy-start.2 = (bf16[1,8,16,16,256]{4,3,2,1,0:T(8,128)(2,1)}, bf16[1,8,16,16,256]{4,3,2,1,0:T(8,128)(2,1)S(1)}, u32[]{:S(2)}) copy-start(bf16[1,8,16,16,256]{4,3,2,1,0:T(8,128)(2,1)S(1)} %copy.76) | copy-start | bytes 3145732
  76.5 1.1 copy-start.1
  110.4 1.2 copy-start.7
  114.1 1.6 copy-start.5
  117.5 31.0 %copy-start.3 = (bf16[1,8,16,16,256]{4,3,2,1,0:T(8,128)(2,1)S(1)}, bf16[1,8,16,16,256]{4,3,2,1,0:T(8,128)(2,1)}, u32[]{:S(2)}) copy-start(bf16[1,8,16,16,256]{4,3,2,1,0:T(8,128)(2,1)} %copy-done.2) | copy-start | bytes 3145732
  147.3 1.0 copy-start.4
  150.6 28.0 %all-to-all-start.4 = ((bf16[1,8,256,256]{3,1,0,2:T(8,128)(2,1)}), bf16[1,8,256,256]{3,1,0,2:T(8,128)(2,1)}, u32[]{:S(2)}, u32[]{:S(2)}) async-start(bf16[1,8,256,256]{3,1,0,2:T(8,128)(2,1)} %copy.84), calls=%async_computation.4 | async-start | bytes 2097152 | tf_op jit(solution)/shard_map/all_to_all | solution.py:98
  178.6 29.9 %all-to-all-start.5 = ((bf16[1,8,256,256]{3,1,0,2:T(8,128)(2,1)}), bf16[1,8,256,256]{3,1,0,2:T(8,128)(2,1)}, u32[]{:S(2)}, u32[]{:S(2)}) async-start(bf16[1,8,256,256]{3,1,0,2:T(8,128)(2,1)} %copy.87), calls=%async_computation.5 | async-start | bytes 2097152 | tf_op jit(solution)/shard_map/all_to_all | solution.py:99
  185.5 124.0 %all-reduce.2.cloned.1.call-start = ((), (), s32[]{:S(2)}) async-start(), calls=%async_computation.6 | async-start | bytes 393216 | tf_op jit(solution)/shard_map/psum | solution.py:121
  185.8 2.0 copy-start.6
  214.8 1.2 copy-start.8
Sparse Core Ops, SparseCore 0:
  217.6 91.8 all-reduce.1
where the time goes:
time: 319 us; the launch traced here: 318 us
  waiting for transfers between devices  170 us (53%)
  blocking collectives  61.3 us (19%)
  starting transfers between devices  26.5 us (8%)
  local copies, waits for them, and re-layouts  16.9 us (5%)
  matrix products  16.5 us (5%)
  between operations  14.4 us (5%)
  other arithmetic  12.6 us (4%)
    psum x1, waiting for transfers between devices, body(): lax.psum(jnp.concatenate([in_weights, out_weights], axis=0).astype(jnp.bf...  88.2 us
    all_to_all x1, blocking collectives, body(): lax.all_to_all(products, 'rows', split_axis=2, concat_axis=0, tiled=True)  31.5 us
    all_to_all x1, blocking collectives, body(): lax.all_to_all(prod_grad, 'rows', split_axis=0, concat_axis=2, tiled=True)  29.8 us
    all_to_all x1, waiting for transfers between devices, body(): lax.all_to_all(left_edge, 'rows', split_axis=0, concat_axis=2, tiled=True)  22.8 us
    all_to_all x1, waiting for transfers between devices, body(): lax.all_to_all(right_edge, 'rows', split_axis=0, concat_axis=2, tiled=True)  21.9 us
    all_to_all x1, waiting for transfers between devices, body(): lax.all_to_all(left_part, 'rows', split_axis=2, concat_axis=0, tiled=True)  19.3 us
    all_to_all x1, waiting for transfers between devices, body(): lax.all_to_all(right_part, 'rows', split_axis=2, concat_axis=0, tiled=True)  17.8 us
    unnamed x23, local copies, waits for them, and re-layouts  8.91 us
  transfers between devices with their start and end apart: 5, of which 5 were waited for; matrix products, arithmetic and copies ran while one was open for 4% of the time, Pallas kernels for 0%

commit v1 on v0

--- a/solution.py
+++ b/solution.py
@@ -2,6 +2,22 @@
 import jax.numpy as jnp
 from jax import lax
 from jax.sharding import PartitionSpec as P
+
+
+def exchange_in_pairs(x, axis, split, join):
+    ways, here = (lax.axis_size(axis), lax.axis_index(axis))
+    width = x.shape[split] // ways
+    shape = list(x.shape)
+    shape[split] = width
+    height = shape[join]
+    shape[join] = height * ways
+    full = jnp.zeros(shape, x.dtype)
+    for mask in range(ways):
+        part = lax.dynamic_slice_in_dim(x, (here ^ mask) * width, width, axis=split)
+        if mask:
+            part = lax.ppermute(part, axis, [(d, d ^ mask) for d in range(ways)])
+        full = lax.dynamic_update_slice_in_dim(full, part, (here ^ mask) * height, axis=join)
+    return full
 
 
 def layer_norm(values, along_dim):
@@ -96,7 +112,7 @@
     left_part, right_part = edge_backward(slab_grad, left_held, right_held)
     left_back, right_back = (
         lax.all_to_all(left_part, "rows", split_axis=2, concat_axis=0, tiled=True),
-        lax.all_to_all(right_part, "rows", split_axis=2, concat_axis=0, tiled=True),
+        exchange_in_pairs(right_part, "rows", 2, 0),
     )
     left_full = left_back.reshape(chans, local_rows, residues).astype(jnp.float32)
     right_full = right_back.reshape(chans, local_rows, residues).astype(jnp.float32)

time: 319 us -> 334 us (1.047)
  waiting for transfers between devices: 170 us -> 201 us
  blocking collectives: 61.3 us -> 31.5 us
  starting transfers between devices: 26.5 us -> 40 us
    ppermute x0 -> x15, waiting for transfers between devices: none -> 53.6 us  [exchange_in_pairs(): part = lax.ppermute(part, axis, [(d, d ^ mask) for d in range(ways)])]
    all_to_all x1 -> x0, blocking collectives: 29.8 us -> none  [body(): lax.all_to_all(prod_grad, 'rows', split_axis=0, concat_axis=2, tiled=True)]
    all_to_all x1, waiting for transfers between devices: 19.3 us -> 0.01 us  [body(): lax.all_to_all(left_part, 'rows', split_axis=2, concat_axis=0, tiled=True)]
    ppermute x0 -> x15, starting transfers between devices: none -> 13.8 us  [exchange_in_pairs(): part = lax.ppermute(part, axis, [(d, d ^ mask) for d in range(ways)])]
    unnamed x23 -> x21, local copies, waits for them, and re-layouts: 8.91 us -> 7.89 us
  transfers between devices with their start and end apart: 5 -> 20, of which waited for: 5 -> 15; matrix products, arithmetic and copies ran while one was open for 4% -> 3% of each run, Pallas kernels for 0% -> 0%
where the time goes in v1:
time: 334 us; the launch traced here: 333 us
  waiting for transfers between devices  201 us (60%)
  starting transfers between devices  40 us (12%)
  blocking collectives  31.5 us (9%)
  local copies, waits for them, and re-layouts  17.2 us (5%)
  matrix products  16.6 us (5%)
  between operations  14.8 us (4%)
  other arithmetic  12.1 us (4%)
    psum x1, waiting for transfers between devices, body(): lax.psum(jnp.concatenate([in_weights, out_weights], axis=0).astype(jnp.bf...  85.1 us
    ppermute x15, waiting for transfers between devices, exchange_in_pairs(): part = lax.ppermute(part, axis, [(d, d ^ mask) for d in range(ways)])  53.6 us
    all_to_all x1, blocking collectives, body(): lax.all_to_all(products, 'rows', split_axis=2, concat_axis=0, tiled=True)  31.5 us
    all_to_all x1, waiting for transfers between devices, body(): lax.all_to_all(left_edge, 'rows', split_axis=0, concat_axis=2, tiled=True)  22.8 us
    all_to_all x1, waiting for transfers between devices, body(): lax.all_to_all(right_edge, 'rows', split_axis=0, concat_axis=2, tiled=True)  21.9 us
    all_to_all x1, waiting for transfers between devices, body(): lax.all_to_all(prod_grad, 'rows', split_axis=0, concat_axis=2, tiled=True)  17.9 us
    ppermute x15, starting transfers between devices, exchange_in_pairs(): part = lax.ppermute(part, axis, [(d, d ^ mask) for d in range(ways)])  13.8 us
    unnamed x21, local copies, waits for them, and re-layouts  7.89 us
  transfers between devices with their start and end apart: 20, of which 15 were waited for; matrix products, arithmetic and copies ran while one was open for 3% of the time, Pallas kernels for 0%

profile of v1, /device:TPU:0, one launch (start us, length us, event | category | flops | bytes accessed | tf_op | source)
XLA Modules:
  0.0 333.5 jit_solution(10166912345963689288)
XLA Ops:
  14.8 7.4 %all-to-all-start.1 = ((bf16[16,8,16,256]{3,1,2,0:T(8,128)(2,1)}), bf16[16,8,16,256]{3,1,2,0:T(8,128)(2,1)S(1)}, u32[]{:S(2)}, u32[]{:S(2)}) async-start(bf16[16,8,16,256]{3,1,2,0:T(8,128)(2,1)} %copy.103), calls=%async_computation.1 | async-start | bytes 2097152 | tf_op jit(solution)/shard_map/all_to_all | solution.py:84
  23.3 21.9 %all-to-all-done.1 = bf16[16,8,16,256]{3,1,2,0:T(8,128)(2,1)S(1)} async-done(((bf16[16,8,16,256]{3,1,2,0:T(8,128)(2,1)}), bf16[16,8,16,256]{3,1,2,0:T(8,128)(2,1)S(1)}, u32[]{:S(2)}, u32[]{:S(2)}) %all-to-all-start.1) | async-done | bytes 1048608 | tf_op jit(solution)/shard_map/all_to_all | solution.py:84
  45.2 6.9 %all-to-all-start = ((bf16[16,8,16,256]{3,1,2,0:T(8,128)(2,1)}), bf16[16,8,16,256]{3,1,2,0:T(8,128)(2,1)}, u32[]{:S(2)}, u32[]{:S(2)}) async-start(bf16[16,8,16,256]{3,1,2,0:T(8,128)(2,1)} %copy.101), calls=%async_computation | async-start | bytes 2097152 | tf_op jit(solution)/shard_map/all_to_all | solution.py:83
  52.3 22.8 %all-to-all-done = bf16[16,8,16,256]{3,1,2,0:T(8,128)(2,1)} async-done(((bf16[16,8,16,256]{3,1,2,0:T(8,128)(2,1)}), bf16[16,8,16,256]{3,1,2,0:T(8,128)(2,1)}, u32[]{:S(2)}, u32[]{:S(2)}) %all-to-all-start) | async-done | bytes 1048608 | tf_op jit(solution)/shard_map/all_to_all | solution.py:83
  77.6 31.5 %all_to_all.63 = bf16[1,8,256,256]{3,1,0,2:T(8,128)(2,1)S(1)} all-to-all(bf16[1,8,256,256]{3,1,0,2:T(8,128)(2,1)S(1)} %copy.105), channel_id=1, replica_groups=mesh['groups'=2,'rows'=16] {'rows'}, dimensions={2} | all-to-all | bytes 2097152 | tf_op jit(solution)/shard_map/all_to_all | solution.py:87
  111.6 2.5 fusion.13
  118.5 5.0 %all-to-all-start.3 = ((bf16[16,8,16,256]{3,1,2,0:T(8,128)(2,1)}), bf16[16,8,16,256]{3,1,2,0:T(8,128)(2,1)}, u32[]{:S(2)}, u32[]{:S(2)}) async-start(bf16[16,8,16,256]{3,1,2,0:T(8,128)(2,1)} %copy.110), calls=%async_computation.3 | async-start | bytes 2097152 | tf_op jit(solution)/shard_map/all_to_all | solution.py:111
  125.8 2.9 fusion.41
  128.7 17.9 %all-to-all-done.3 = bf16[16,8,16,256]{3,1,2,0:T(8,128)(2,1)} async-done(((bf16[16,8,16,256]{3,1,2,0:T(8,128)(2,1)}), bf16[16,8,16,256]{3,1,2,0:T(8,128)(2,1)}, u32[]{:S(2)}, u32[]{:S(2)}) %all-to-all-start.3) | async-done | bytes 1048608 | tf_op jit(solution)/shard_map/all_to_all | solution.py:111
  152.2 6.9 %all-to-all-start.4 = ((bf16[1,8,256,256]{3,1,0,2:T(8,128)(2,1)}), bf16[1,8,256,256]{3,1,0,2:T(8,128)(2,1)S(1)}, u32[]{:S(2)}, u32[]{:S(2)}) async-start(bf16[1,8,256,256]{3,1,0,2:T(8,128)(2,1)} %copy.112), calls=%async_computation.4 | async-start | bytes 2097152 | tf_op jit(solution)/shard_map/all_to_all | solution.py:114
  159.3 4.4 %collective-permute-start.14 = (bf16[1,8,16,256]{3,2,1,0:T(8,128)(2,1)S(1)}, bf16[1,8,16,256]{3,2,1,0:T(8,128)(2,1)S(1)}, u32[]{:S(2)}, u32[]{:S(2)}) collective-permute-start(bf16[1,8,16,256]{3,2,1,0:T(8,128)(2,1)S(1)} %get-tuple-element.29), channel_id=1, source_target_pairs={{0,15},{1,14},{2,13},{3,12},{4,11},{5,10},{6,9},{7,8},{8,7},{9,6},... | collective-permute-start | bytes 196616 | tf_op jit(solution)/shard_map/ppermute | solution.py:18
  164.2 3.1 collective-permute-start.12
  170.6 4.1 %collective-permute-done.1 = bf16[1,8,16,256]{3,2,1,0:T(8,128)(2,1)S(1)} collective-permute-done((bf16[1,8,16,256]{3,2,1,0:T(8,128)(2,1)S(1)}, bf16[1,8,16,256]{3,2,1,0:T(8,128)(2,1)S(1)}, u32[]{:S(2)}, u32[]{:S(2)}) %collective-permute-start.1) | collective-permute-done | bytes 65568 | tf_op jit(solution)/shard_map/ppermute | solution.py:18
  174.7 4.3 %collective-permute-done.2 = bf16[1,8,16,256]{3,2,1,0:T(8,128)(2,1)S(1)} collective-permute-done((bf16[1,8,16,256]{3,2,1,0:T(8,128)(2,1)S(1)}, bf16[1,8,16,256]{3,2,1,0:T(8,128)(2,1)S(1)}, u32[]{:S(2)}, u32[]{:S(2)}) %collective-permute-start.2) | collective-permute-done | bytes 65568 | tf_op jit(solution)/shard_map/ppermute | solution.py:18
  179.0 10.9 %collective-permute-done.3 = bf16[1,8,16,256]{3,2,1,0:T(8,128)(2,1)S(1)} collective-permute-done((bf16[1,8,16,256]{3,2,1,0:T(8,128)(2,1)S(1)}, bf16[1,8,16,256]{3,2,1,0:T(8,128)(2,1)S(1)}, u32[]{:S(2)}, u32[]{:S(2)}) %collective-permute-start.3) | collective-permute-done | bytes 65568 | tf_op jit(solution)/shard_map/ppermute | solution.py:18
  189.9 4.1 %collective-permute-done.4 = bf16[1,8,16,256]{3,2,1,0:T(8,128)(2,1)S(1)} collective-permute-done((bf16[1,8,16,256]{3,2,1,0:T(8,128)(2,1)S(1)}, bf16[1,8,16,256]{3,2,1,0:T(8,128)(2,1)S(1)}, u32[]{:S(2)}, u32[]{:S(2)}) %collective-permute-start.4) | collective-permute-done | bytes 65568 | tf_op jit(solution)/shard_map/ppermute | solution.py:18
  194.8 4.5 %collective-permute-done.5 = bf16[1,8,16,256]{3,2,1,0:T(8,128)(2,1)S(1)} collective-permute-done((bf16[1,8,16,256]{3,2,1,0:T(8,128)(2,1)S(1)}, bf16[1,8,16,256]{3,2,1,0:T(8,128)(2,1)S(1)}, u32[]{:S(2)}, u32[]{:S(2)}) %collective-permute-start.5) | collective-permute-done | bytes 65568 | tf_op jit(solution)/shard_map/ppermute | solution.py:18
  199.4 4.4 %collective-permute-done.6 = bf16[1,8,16,256]{3,2,1,0:T(8,128)(2,1)S(1)} collective-permute-done((bf16[1,8,16,256]{3,2,1,0:T(8,128)(2,1)S(1)}, bf16[1,8,16,256]{3,2,1,0:T(8,128)(2,1)S(1)}, u32[]{:S(2)}, u32[]{:S(2)}) %collective-permute-start.6) | collective-permute-done | bytes 65568 | tf_op jit(solution)/shard_map/ppermute | solution.py:18
  205.1 4.5 %collective-permute-done.7 = bf16[1,8,16,256]{3,2,1,0:T(8,128)(2,1)S(1)} collective-permute-done((bf16[1,8,16,256]{3,2,1,0:T(8,128)(2,1)S(1)}, bf16[1,8,16,256]{3,2,1,0:T(8,128)(2,1)S(1)}, u32[]{:S(2)}, u32[]{:S(2)}) %collective-permute-start.7) | collective-permute-done | bytes 65568 | tf_op jit(solution)/shard_map/ppermute | solution.py:18
  209.6 5.3 %collective-permute-done.8 = bf16[1,8,16,256]{3,2,1,0:T(8,128)(2,1)S(1)} collective-permute-done((bf16[1,8,16,256]{3,2,1,0:T(8,128)(2,1)S(1)}, bf16[1,8,16,256]{3,2,1,0:T(8,128)(2,1)S(1)}, u32[]{:S(2)}, u32[]{:S(2)}) %collective-permute-start.8) | collective-permute-done | bytes 65568 | tf_op jit(solution)/shard_map/ppermute | solution.py:18
  216.5 4.5 %collective-permute-done.9 = bf16[1,8,16,256]{3,2,1,0:T(8,128)(2,1)S(1)} collective-permute-done((bf16[1,8,16,256]{3,2,1,0:T(8,128)(2,1)S(1)}, bf16[1,8,16,256]{3,2,1,0:T(8,128)(2,1)S(1)}, u32[]{:S(2)}, u32[]{:S(2)}) %collective-permute-start.9) | collective-permute-done | bytes 65568 | tf_op jit(solution)/shard_map/ppermute | solution.py:18
  221.1 6.1 %collective-permute-done.10 = bf16[1,8,16,256]{3,2,1,0:T(8,128)(2,1)S(1)} collective-permute-done((bf16[1,8,16,256]{3,2,1,0:T(8,128)(2,1)S(1)}, bf16[1,8,16,256]{3,2,1,0:T(8,128)(2,1)S(1)}, u32[]{:S(2)}, u32[]{:S(2)}) %collective-permute-start.10) | collective-permute-done | bytes 65568 | tf_op jit(solution)/shard_map/ppermute | solution.py:18
  227.4 4.4 %fusion.24 = (bf16[1,128,16,256]{3,1,0,2:T(8,128)(2,1)S(1)}, bf16[1,128,16,256]{3,1,0,2:T(8,128)(2,1)S(1)}, bf16[1,128,16,256]{3,1,0,2:T(8,128)(2,1)S(1)}, bf16[1,128,16,256]{3,1,0,2:T(8,128)(2,1)S(1)}) fusion(f32[4,128,16,256]{3,1,0,2:T(8,128)} %copy-done, bf16[16,8,16,256]{3,1,0,2:T(8,128)(2,1)S(1)} %copy_dynamic-update-slice_fusion, ...), kind=kLoop, calls=%fused_computation.37 | loop fusion | flops 11534336 | bytes 14680064 | tf_op jit(solution)/shard_map/convert.15
  239.6 85.1 %all-reduce.2.cloned.1.call-done = bf16[6,128,128]{1,2,0:T(8,128)(2,1)} async-done(((bf16[6,128,128]{1,2,0:T(8,128)(2,1)}), bf16[6,128,128]{1,2,0:T(8,128)(2,1)}) %all-reduce.2.cloned.1.call-update) | async-done | bytes 196624 | tf_op jit(solution)/shard_map/psum | solution.py:137
  (97 shorter events, 43.3 us)
Async XLA Ops:
  7.2 2.1 copy-start.8
  10.5 3.2 copy-start
  14.8 30.3 %all-to-all-start.1 = ((bf16[16,8,16,256]{3,1,2,0:T(8,128)(2,1)}), bf16[16,8,16,256]{3,1,2,0:T(8,128)(2,1)S(1)}, u32[]{:S(2)}, u32[]{:S(2)}) async-start(bf16[16,8,16,256]{3,1,2,0:T(8,128)(2,1)} %copy.103), calls=%async_computation.1 | async-start | bytes 2097152 | tf_op jit(solution)/shard_map/all_to_all | solution.py:84
  45.2 29.9 %all-to-all-start = ((bf16[16,8,16,256]{3,1,2,0:T(8,128)(2,1)}), bf16[16,8,16,256]{3,1,2,0:T(8,128)(2,1)}, u32[]{:S(2)}, u32[]{:S(2)}) async-start(bf16[16,8,16,256]{3,1,2,0:T(8,128)(2,1)} %copy.101), calls=%async_computation | async-start | bytes 2097152 | tf_op jit(solution)/shard_map/all_to_all | solution.py:83
  52.3 24.7 %copy-start.1 = (bf16[1,8,16,16,256]{4,3,2,1,0:T(8,128)(2,1)}, bf16[1,8,16,16,256]{4,3,2,1,0:T(8,128)(2,1)S(1)}, u32[]{:S(2)}) copy-start(bf16[1,8,16,16,256]{4,3,2,1,0:T(8,128)(2,1)S(1)} %copy.104) | copy-start | bytes 3145732
  118.5 28.0 %all-to-all-start.3 = ((bf16[16,8,16,256]{3,1,2,0:T(8,128)(2,1)}), bf16[16,8,16,256]{3,1,2,0:T(8,128)(2,1)}, u32[]{:S(2)}, u32[]{:S(2)}) async-start(bf16[16,8,16,256]{3,1,2,0:T(8,128)(2,1)} %copy.110), calls=%async_computation.3 | async-start | bytes 2097152 | tf_op jit(solution)/shard_map/all_to_all | solution.py:111
  146.6 3.6 %copy-start.2 = (bf16[1,8,16,16,256]{4,3,2,1,0:T(8,128)(2,1)S(1)}, bf16[1,8,16,16,256]{4,3,2,1,0:T(8,128)(2,1)}, u32[]{:S(2)}) copy-start(bf16[1,8,16,16,256]{4,3,2,1,0:T(8,128)(2,1)} %copy-done.1) | copy-start | bytes 3145732
  152.2 75.1 %all-to-all-start.4 = ((bf16[1,8,256,256]{3,1,0,2:T(8,128)(2,1)}), bf16[1,8,256,256]{3,1,0,2:T(8,128)(2,1)S(1)}, u32[]{:S(2)}, u32[]{:S(2)}) async-start(bf16[1,8,256,256]{3,1,0,2:T(8,128)(2,1)} %copy.112), calls=%async_computation.4 | async-start | bytes 2097152 | tf_op jit(solution)/shard_map/all_to_all | solution.py:114
  159.1 165.6 %all-reduce.2.cloned.1.call-start = ((), (), s32[]{:S(2)}) async-start(), calls=%async_computation.5 | async-start | bytes 393216 | tf_op jit(solution)/shard_map/psum | solution.py:137
  159.3 68.0 %collective-permute-start.14 = (bf16[1,8,16,256]{3,2,1,0:T(8,128)(2,1)S(1)}, bf16[1,8,16,256]{3,2,1,0:T(8,128)(2,1)S(1)}, u32[]{:S(2)}, u32[]{:S(2)}) collective-permute-start(bf16[1,8,16,256]{3,2,1,0:T(8,128)(2,1)S(1)} %get-tuple-element.29), channel_id=1, source_target_pairs={{0,15},{1,14},{2,13},{3,12},{4,11},{5,10},{6,9},{7,8},{8,7},{9,6},... | collective-permute-start | bytes 196616 | tf_op jit(solution)/shard_map/ppermute | solution.py:18
  163.8 63.5 %collective-permute-start.13 = (bf16[1,8,16,256]{3,2,1,0:T(8,128)(2,1)S(1)}, bf16[1,8,16,256]{3,2,1,0:T(8,128)(2,1)S(1)}, u32[]{:S(2)}, u32[]{:S(2)}) collective-permute-start(bf16[1,8,16,256]{3,2,1,0:T(8,128)(2,1)S(1)} %get-tuple-element.30), channel_id=1, source_target_pairs={{0,14},{1,15},{2,12},{3,13},{4,10},{5,11},{6,8},{7,9},{8,6},{9,7},... | collective-permute-start | bytes 196616 | tf_op jit(solution)/shard_map/ppermute | solution.py:18
  164.2 63.1 %collective-permute-start.12 = (bf16[1,8,16,256]{3,2,1,0:T(8,128)(2,1)S(1)}, bf16[1,8,16,256]{3,2,1,0:T(8,128)(2,1)S(1)}, u32[]{:S(2)}, u32[]{:S(2)}) collective-permute-start(bf16[1,8,16,256]{3,2,1,0:T(8,128)(2,1)S(1)} %get-tuple-element.31), channel_id=1, source_target_pairs={{0,13},{1,12},{2,15},{3,14},{4,9},{5,8},{6,11},{7,10},{8,5},{9,4},... | collective-permute-start | bytes 196616 | tf_op jit(solution)/shard_map/ppermute | solution.py:18
  167.3 59.9 %collective-permute-start.11 = (bf16[1,8,16,256]{3,2,1,0:T(8,128)(2,1)S(1)}, bf16[1,8,16,256]{3,2,1,0:T(8,128)(2,1)S(1)}, u32[]{:S(2)}, u32[]{:S(2)}) collective-permute-start(bf16[1,8,16,256]{3,2,1,0:T(8,128)(2,1)S(1)} %get-tuple-element.32), channel_id=1, source_target_pairs={{0,12},{1,13},{2,14},{3,15},{4,8},{5,9},{6,10},{7,11},{8,4},{9,5},... | collective-permute-start | bytes 196616 | tf_op jit(solution)/shard_map/ppermute | solution.py:18
  167.6 1.3 collective-permute-start
  168.9 5.8 %collective-permute-start.1 = (bf16[1,8,16,256]{3,2,1,0:T(8,128)(2,1)S(1)}, bf16[1,8,16,256]{3,2,1,0:T(8,128)(2,1)S(1)}, u32[]{:S(2)}, u32[]{:S(2)}) collective-permute-start(bf16[1,8,16,256]{3,2,1,0:T(8,128)(2,1)S(1)} %get-tuple-element.42), channel_id=1, source_target_pairs={{0,2},{1,3},{2,0},{3,1},{4,6},{5,7},{6,4},{7,5},{8,10},{9,11},{10,... | collective-permute-start | bytes 196616 | tf_op jit(solution)/shard_map/ppermute | solution.py:18
  174.7 4.3 %collective-permute-start.2 = (bf16[1,8,16,256]{3,2,1,0:T(8,128)(2,1)S(1)}, bf16[1,8,16,256]{3,2,1,0:T(8,128)(2,1)S(1)}, u32[]{:S(2)}, u32[]{:S(2)}) collective-permute-start(bf16[1,8,16,256]{3,2,1,0:T(8,128)(2,1)S(1)} %get-tuple-element.41), channel_id=1, source_target_pairs={{0,3},{1,2},{2,1},{3,0},{4,7},{5,6},{6,5},{7,4},{8,11},{9,10},{10,... | collective-permute-start | bytes 196616 | tf_op jit(solution)/shard_map/ppermute | solution.py:18
  179.0 10.9 %collective-permute-start.3 = (bf16[1,8,16,256]{3,2,1,0:T(8,128)(2,1)S(1)}, bf16[1,8,16,256]{3,2,1,0:T(8,128)(2,1)S(1)}, u32[]{:S(2)}, u32[]{:S(2)}) collective-permute-start(bf16[1,8,16,256]{3,2,1,0:T(8,128)(2,1)S(1)} %get-tuple-element.40), channel_id=1, source_target_pairs={{0,4},{1,5},{2,6},{3,7},{4,0},{5,1},{6,2},{7,3},{8,12},{9,13},{10,... | collective-permute-start | bytes 196616 | tf_op jit(solution)/shard_map/ppermute | solution.py:18
  189.9 4.2 %collective-permute-start.4 = (bf16[1,8,16,256]{3,2,1,0:T(8,128)(2,1)S(1)}, bf16[1,8,16,256]{3,2,1,0:T(8,128)(2,1)S(1)}, u32[]{:S(2)}, u32[]{:S(2)}) collective-permute-start(bf16[1,8,16,256]{3,2,1,0:T(8,128)(2,1)S(1)} %get-tuple-element.39), channel_id=1, source_target_pairs={{0,5},{1,4},{2,7},{3,6},{4,1},{5,0},{6,3},{7,2},{8,13},{9,12},{10,... | collective-permute-start | bytes 196616 | tf_op jit(solution)/shard_map/ppermute | solution.py:18
  194.1 5.2 %collective-permute-start.5 = (bf16[1,8,16,256]{3,2,1,0:T(8,128)(2,1)S(1)}, bf16[1,8,16,256]{3,2,1,0:T(8,128)(2,1)S(1)}, u32[]{:S(2)}, u32[]{:S(2)}) collective-permute-start(bf16[1,8,16,256]{3,2,1,0:T(8,128)(2,1)S(1)} %get-tuple-element.38), channel_id=1, source_target_pairs={{0,6},{1,7},{2,4},{3,5},{4,2},{5,3},{6,0},{7,1},{8,14},{9,15},{10,... | collective-permute-start | bytes 196616 | tf_op jit(solution)/shard_map/ppermute | solution.py:18
  199.2 4.6 %collective-permute-start.6 = (bf16[1,8,16,256]{3,2,1,0:T(8,128)(2,1)S(1)}, bf16[1,8,16,256]{3,2,1,0:T(8,128)(2,1)S(1)}, u32[]{:S(2)}, u32[]{:S(2)}) collective-permute-start(bf16[1,8,16,256]{3,2,1,0:T(8,128)(2,1)S(1)} %get-tuple-element.37), channel_id=1, source_target_pairs={{0,7},{1,6},{2,5},{3,4},{4,3},{5,2},{6,1},{7,0},{8,15},{9,14},{10,... | collective-permute-start | bytes 196616 | tf_op jit(solution)/shard_map/ppermute | solution.py:18
  203.8 5.8 %collective-permute-start.7 = (bf16[1,8,16,256]{3,2,1,0:T(8,128)(2,1)S(1)}, bf16[1,8,16,256]{3,2,1,0:T(8,128)(2,1)S(1)}, u32[]{:S(2)}, u32[]{:S(2)}) collective-permute-start(bf16[1,8,16,256]{3,2,1,0:T(8,128)(2,1)S(1)} %get-tuple-element.36), channel_id=1, source_target_pairs={{0,8},{1,9},{2,10},{3,11},{4,12},{5,13},{6,14},{7,15},{8,0},{9,1},... | collective-permute-start | bytes 196616 | tf_op jit(solution)/shard_map/ppermute | solution.py:18
  209.6 5.4 %collective-permute-start.8 = (bf16[1,8,16,256]{3,2,1,0:T(8,128)(2,1)S(1)}, bf16[1,8,16,256]{3,2,1,0:T(8,128)(2,1)S(1)}, u32[]{:S(2)}, u32[]{:S(2)}) collective-permute-start(bf16[1,8,16,256]{3,2,1,0:T(8,128)(2,1)S(1)} %get-tuple-element.35), channel_id=1, source_target_pairs={{0,9},{1,8},{2,11},{3,10},{4,13},{5,12},{6,15},{7,14},{8,1},{9,0},... | collective-permute-start | bytes 196616 | tf_op jit(solution)/shard_map/ppermute | solution.py:18
  215.0 6.1 %collective-permute-start.9 = (bf16[1,8,16,256]{3,2,1,0:T(8,128)(2,1)S(1)}, bf16[1,8,16,256]{3,2,1,0:T(8,128)(2,1)S(1)}, u32[]{:S(2)}, u32[]{:S(2)}) collective-permute-start(bf16[1,8,16,256]{3,2,1,0:T(8,128)(2,1)S(1)} %get-tuple-element.34), channel_id=1, source_target_pairs={{0,10},{1,11},{2,8},{3,9},{4,14},{5,15},{6,12},{7,13},{8,2},{9,3},... | collective-permute-start | bytes 196616 | tf_op jit(solution)/shard_map/ppermute | solution.py:18
  221.0 6.1 %collective-permute-start.10 = (bf16[1,8,16,256]{3,2,1,0:T(8,128)(2,1)S(1)}, bf16[1,8,16,256]{3,2,1,0:T(8,128)(2,1)S(1)}, u32[]{:S(2)}, u32[]{:S(2)}) collective-permute-start(bf16[1,8,16,256]{3,2,1,0:T(8,128)(2,1)S(1)} %get-tuple-element.33), channel_id=1, source_target_pairs={{0,11},{1,10},{2,9},{3,8},{4,15},{5,14},{6,13},{7,12},{8,3},{9,2},... | collective-permute-start | bytes 196616 | tf_op jit(solution)/shard_map/ppermute | solution.py:18
  (5 other events, 7.1 us)
Sparse Core Ops, SparseCore 0:
  235.9 88.8 all-reduce.1
